TPU v7x, 512 devices: a whole 4x8x8 slice. The times are simulated.
512 devices in a mesh: space: 32 (over y, z_lo), mode: 16 (over x, z_hi, core).
Axes of the slice: x: 4, y: 8, z: 8 (z_hi: 2, z_lo: 4; z = z_hi * 4 + z_lo), core: 2. Of those that a mesh axis runs over, the one named last changes fastest.
Arguments:
- old_modes: bfloat16 [512, 64, 4096], P('mode', None, 'space'), as said below
- new_modes: bfloat16 [512, 64, 4096], P('mode', None, 'space'), as said below
- material: int32 [64, 4096], P(None, 'space'), may hold values from 0 to 11
- density: float32 [12], replicated, may hold values from 0.5 to 2
- memb_x: bfloat16 [12], replicated, may hold values from 1 to 4
- memb_y: bfloat16 [12], replicated, may hold values from 1 to 4
- bend_table: float32 [12], replicated, may hold values from 0.02 to 0.1
Outputs:
- cross_mass: float32 [512, 512], P(None, 'mode')
- cross_membrane: float32 [512, 512], P(None, 'mode')
- cross_bending: float32 [512, 512], P(None, 'mode')
- mass_image: bfloat16 [512, 64, 4096], P('mode', None, 'space')
- stiff_image: bfloat16 [512, 64, 4096], P('mode', None, 'space')
Inputs may be any that keep to these rules, and one draw needn't show every extreme that they name: `old_modes`: A value of one mode shape at one cell. `new_modes`: A value of one mode shape at one cell.
All inputs are finite; a program needn't handle non-finite values.
Results may differ from a plain program's by a relative error of at most 0.0015.
Values may be sent and summed in bfloat16 or wider, within the bound.
No kernel may reach another device: no remote copies, remote signals or barrier semaphores. Data moves between devices by JAX's collectives and lax.ppermute only.
A program may use at most 64 MiB of HBM per device.

v0:
```python
import jax
import jax.numpy as jnp
from jax import lax
from jax.sharding import PartitionSpec as P


def extended(shard, sides, width):
    for axis, dim in sides:
        devices, length = (lax.axis_size(axis), shard.shape[dim])
        up = [(i, (i + 1) % devices) for i in range(devices - 1)]
        down = [(j, i) for i, j in up]
        last = lax.slice_in_dim(shard, length - width, length, axis=dim)
        initial = lax.slice_in_dim(shard, 0, width, axis=dim)
        before = lax.ppermute(last, axis, up)
        after = lax.ppermute(initial, axis, down)
        shard = jnp.concatenate([before, shard, after], axis=dim)
    return shard


def passed_along(value, axis, steps):
    count = lax.axis_size(axis)
    pairs = [(source, (source + steps) % count) for source in range(count)]
    return lax.ppermute(value, axis, pairs)


def lookup(material, table):
    levels = jnp.arange(table.shape[0], dtype=jnp.int32)
    picks = (material[None, :, :] == levels[:, None, None]).astype(jnp.float32)
    return jnp.sum(picks * table.astype(jnp.float32)[:, None, None], axis=0)


def operators(padded, kxp, kyp, density_field, bend_field, rows, cols):

    def moved(a, b):
        return padded[:, 2 + a : 2 + a + rows, 2 + b : 2 + b + cols]

    center = moved(0, 0)
    east = moved(1, 0)
    west = moved(-1, 0)
    north = moved(0, 1)
    south = moved(0, -1)
    nearest = east + west + north + south
    mass = density_field * (2.0 / 3.0 * center + nearest / 12.0)
    face_e = 0.5 * (kxp[1:-1, 1:-1] + kxp[2:, 1:-1])
    face_w = 0.5 * (kxp[1:-1, 1:-1] + kxp[:-2, 1:-1])
    face_n = 0.5 * (kyp[1:-1, 1:-1] + kyp[1:-1, 2:])
    face_s = 0.5 * (kyp[1:-1, 1:-1] + kyp[1:-1, :-2])
    membrane = (
        face_e * (center - east)
        + face_w * (center - west)
        + face_n * (center - north)
        + face_s * (center - south)
    )
    diagonals = moved(1, 1) + moved(1, -1) + moved(-1, 1) + moved(-1, -1)
    distant = moved(2, 0) + moved(-2, 0) + moved(0, 2) + moved(0, -2)
    bending = bend_field * (20.0 * center - 8.0 * nearest + 2.0 * diagonals + distant)
    return (mass, membrane, bending)


def local(old_modes, new_modes, material, density, memb_x, memb_y, bend_table):
    panel_size, rows, cols = new_modes.shape
    density_field = lookup(material, density)
    kxp = jnp.pad(lookup(material, memb_x), 1)
    ky_field = lookup(material, memb_y).astype(jnp.bfloat16)
    bend_field = lookup(material, bend_table)
    stacked = jnp.concatenate([new_modes, ky_field[None]], axis=0)
    rimmed = extended(stacked, (("space", 2),), 2)
    rimmed = jnp.pad(rimmed, ((0, 0), (2, 2), (0, 0)))
    padded = rimmed[:panel_size].astype(jnp.float32)
    kyp = rimmed[panel_size, 1:-1, 1:-1].astype(jnp.float32)
    mass, membrane, bending = operators(padded, kxp, kyp, density_field, bend_field, rows, cols)
    mass_image = mass.astype(jnp.bfloat16)
    stiff_image = (membrane + bending).astype(jnp.bfloat16)
    images = jnp.concatenate([mass, membrane, bending], axis=0).reshape(3 * panel_size, rows * cols)
    index = lax.axis_index("mode")
    loop_size = lax.axis_size("mode")
    area = 1.0 / (rows * cols * lax.axis_size("space"))

    def place(grams, panel, owner):
        block = lax.dot_general(
            panel.reshape(panel_size, rows * cols).astype(jnp.float32),
            images,
            (((1,), (1,)), ((), ())),
            precision=lax.Precision.HIGHEST,
            preferred_element_type=jnp.float32,
        )
        start = jnp.mod(owner, loop_size) * panel_size
        return lax.dynamic_update_slice(grams, block, (start, jnp.int32(0)))

    grams = jnp.zeros((loop_size * panel_size, 3 * panel_size), jnp.float32)
    grams = place(grams, old_modes, index)

    def turn(step, carry):
        panel, totals = carry
        panel = passed_along(panel, "mode", 1)
        return (panel, place(totals, panel, index - step))

    last, grams = lax.fori_loop(1, loop_size, turn, (old_modes, grams))
    total = lax.psum(grams, "space")
    cross_mass = total[:, :panel_size] * area
    cross_membrane = total[:, panel_size : 2 * panel_size] * area
    cross_bending = total[:, 2 * panel_size :] * area
    return (cross_mass, cross_membrane, cross_bending, mass_image, stiff_image)


def solution(mesh):
    in_specs = (
        P("mode", None, "space"),
        P("mode", None, "space"),
        P(None, "space"),
        P(),
        P(),
        P(),
        P(),
    )
    out_specs = (
        P(None, "mode"),
        P(None, "mode"),
        P(None, "mode"),
        P("mode", None, "space"),
        P("mode", None, "space"),
    )
    return jax.shard_map(local, mesh=mesh, in_specs=in_specs, out_specs=out_specs, check_vma=False)
```

profile of v0, /device:TPU:2, one launch (start us, length us, event | category | flops | bytes accessed | tf_op | source)
XLA Modules:
  0.0 738.0 jit_solution(993492930398526759)
XLA Ops:
  13.9 4.9 collective-permute-start.1
  24.7 7.6 %add_convert_fusion = (bf16[32,64,128]{1,0,2:T(8,128)(2,1)}, f32[32,64,128]{1,0,2:T(8,128)S(1)}, f32[32,64,128]{1,0,2:T(8,128)S(1)}, f32[32,64,128]{1,0,2:T(8,128)S(1)}) fusion(f32[32,68,132]{1,0,2:T(8,128)S(1)} %slice_convert_fusion, f32[64,128]{0,1:T(8,128)S(1)} %copy.93, f32[64,128]{0,1:T(8,128)S(1)} %copy.91, f32[64,128]{0,1:T(8,128)S(1)} %copy.88, ...), kind=kLoop, calls=%fused_computation.18 | loop fusion | flops 7602176 | bytes 17465344 | tf_op jit(solution)/shard_map/convert_element_type | solution.py:73
  35.9 3.3 pad_maximum_fusion
  39.2 6.8 copy.97
  46.0 4.3 copy.112
  50.3 5.5 fusion.12
  55.8 336.8 %while.17 = (s32[]{:T(128)}, bf16[32,64,128]{2,1,0:T(8,128)(2,1)}, f32[512,96]{1,0:T(8,128)S(1)}, f32[96,8192]{1,0:T(8,128)S(1)}, s32[]{:T(128)}, /*index=5*/s32...) while((s32[]{:T(128)}, bf16[32,64,128]{2,1,0:T(8,128)(2,1)}, ...), condition=%wide.region_5.6_spmd, body=%wide.region_4.5_spmd.sunk | while | flops 301989920 | bytes 6832448 | solution.py:98
  57.8 14.7 %collective-permute-done = bf16[32,64,128]{2,1,0:T(8,128)(2,1)} collective-permute-done((bf16[32,64,128]{2,1,0:T(8,128)(2,1)}, bf16[32,64,128]{2,1,0:T(8,128)(2,1)}, u32[]{:S(2)}, u32[]{:S(2)}) %collective-permute-start) | collective-permute-done | bytes 524320 | tf_op jit(solution)/shard_map/while/body/eval_jaxpr/ppermute | solution.py:23
  77.2 7.9 %collective-permute-start = (bf16[32,64,128]{2,1,0:T(8,128)(2,1)}, bf16[32,64,128]{2,1,0:T(8,128)(2,1)}, u32[]{:S(2)}, u32[]{:S(2)}) collective-permute-start(bf16[32,64,128]{2,1,0:T(8,128)(2,1)} %get-tuple-element.241), channel_id=1, source_target_pairs={{0,1},{1,2},{2,3},{3,4},{4,5},{5,6},{6,7},{7,8},{8,9},{9,10},{10,1... | collective-permute-start | bytes 1572872 | tf_op jit(solution)/shard_map/while/body/eval_jaxpr/ppermute | solution.py:23
  85.1 7.6 %collective-permute-done = bf16[32,64,128]{2,1,0:T(8,128)(2,1)} collective-permute-done((bf16[32,64,128]{2,1,0:T(8,128)(2,1)}, bf16[32,64,128]{2,1,0:T(8,128)(2,1)}, u32[]{:S(2)}, u32[]{:S(2)}) %collective-permute-start) | collective-permute-done | bytes 524320 | tf_op jit(solution)/shard_map/while/body/eval_jaxpr/ppermute | solution.py:23
  97.4 12.3 %collective-permute-start = (bf16[32,64,128]{2,1,0:T(8,128)(2,1)}, bf16[32,64,128]{2,1,0:T(8,128)(2,1)}, u32[]{:S(2)}, u32[]{:S(2)}) collective-permute-start(bf16[32,64,128]{2,1,0:T(8,128)(2,1)} %get-tuple-element.241), channel_id=1, source_target_pairs={{0,1},{1,2},{2,3},{3,4},{4,5},{5,6},{6,7},{7,8},{8,9},{9,10},{10,1... | collective-permute-start | bytes 1572872 | tf_op jit(solution)/shard_map/while/body/eval_jaxpr/ppermute | solution.py:23
  117.7 12.4 %collective-permute-start = (bf16[32,64,128]{2,1,0:T(8,128)(2,1)}, bf16[32,64,128]{2,1,0:T(8,128)(2,1)}, u32[]{:S(2)}, u32[]{:S(2)}) collective-permute-start(bf16[32,64,128]{2,1,0:T(8,128)(2,1)} %get-tuple-element.241), channel_id=1, source_target_pairs={{0,1},{1,2},{2,3},{3,4},{4,5},{5,6},{6,7},{7,8},{8,9},{9,10},{10,1... | collective-permute-start | bytes 1572872 | tf_op jit(solution)/shard_map/while/body/eval_jaxpr/ppermute | solution.py:23
  137.9 12.5 %collective-permute-start = (bf16[32,64,128]{2,1,0:T(8,128)(2,1)}, bf16[32,64,128]{2,1,0:T(8,128)(2,1)}, u32[]{:S(2)}, u32[]{:S(2)}) collective-permute-start(bf16[32,64,128]{2,1,0:T(8,128)(2,1)} %get-tuple-element.241), channel_id=1, source_target_pairs={{0,1},{1,2},{2,3},{3,4},{4,5},{5,6},{6,7},{7,8},{8,9},{9,10},{10,1... | collective-permute-start | bytes 1572872 | tf_op jit(solution)/shard_map/while/body/eval_jaxpr/ppermute | solution.py:23
  158.2 12.6 %collective-permute-start = (bf16[32,64,128]{2,1,0:T(8,128)(2,1)}, bf16[32,64,128]{2,1,0:T(8,128)(2,1)}, u32[]{:S(2)}, u32[]{:S(2)}) collective-permute-start(bf16[32,64,128]{2,1,0:T(8,128)(2,1)} %get-tuple-element.241), channel_id=1, source_target_pairs={{0,1},{1,2},{2,3},{3,4},{4,5},{5,6},{6,7},{7,8},{8,9},{9,10},{10,1... | collective-permute-start | bytes 1572872 | tf_op jit(solution)/shard_map/while/body/eval_jaxpr/ppermute | solution.py:23
  178.5 12.7 %collective-permute-start = (bf16[32,64,128]{2,1,0:T(8,128)(2,1)}, bf16[32,64,128]{2,1,0:T(8,128)(2,1)}, u32[]{:S(2)}, u32[]{:S(2)}) collective-permute-start(bf16[32,64,128]{2,1,0:T(8,128)(2,1)} %get-tuple-element.241), channel_id=1, source_target_pairs={{0,1},{1,2},{2,3},{3,4},{4,5},{5,6},{6,7},{7,8},{8,9},{9,10},{10,1... | collective-permute-start | bytes 1572872 | tf_op jit(solution)/shard_map/while/body/eval_jaxpr/ppermute | solution.py:23
  198.7 12.8 %collective-permute-start = (bf16[32,64,128]{2,1,0:T(8,128)(2,1)}, bf16[32,64,128]{2,1,0:T(8,128)(2,1)}, u32[]{:S(2)}, u32[]{:S(2)}) collective-permute-start(bf16[32,64,128]{2,1,0:T(8,128)(2,1)} %get-tuple-element.241), channel_id=1, source_target_pairs={{0,1},{1,2},{2,3},{3,4},{4,5},{5,6},{6,7},{7,8},{8,9},{9,10},{10,1... | collective-permute-start | bytes 1572872 | tf_op jit(solution)/shard_map/while/body/eval_jaxpr/ppermute | solution.py:23
  211.5 3.3 collective-permute-done
  219.6 13.3 %collective-permute-start = (bf16[32,64,128]{2,1,0:T(8,128)(2,1)}, bf16[32,64,128]{2,1,0:T(8,128)(2,1)}, u32[]{:S(2)}, u32[]{:S(2)}) collective-permute-start(bf16[32,64,128]{2,1,0:T(8,128)(2,1)} %get-tuple-element.241), channel_id=1, source_target_pairs={{0,1},{1,2},{2,3},{3,4},{4,5},{5,6},{6,7},{7,8},{8,9},{9,10},{10,1... | collective-permute-start | bytes 1572872 | tf_op jit(solution)/shard_map/while/body/eval_jaxpr/ppermute | solution.py:23
  232.9 7.6 %collective-permute-done = bf16[32,64,128]{2,1,0:T(8,128)(2,1)} collective-permute-done((bf16[32,64,128]{2,1,0:T(8,128)(2,1)}, bf16[32,64,128]{2,1,0:T(8,128)(2,1)}, u32[]{:S(2)}, u32[]{:S(2)}) %collective-permute-start) | collective-permute-done | bytes 524320 | tf_op jit(solution)/shard_map/while/body/eval_jaxpr/ppermute | solution.py:23
  245.1 12.7 %collective-permute-start = (bf16[32,64,128]{2,1,0:T(8,128)(2,1)}, bf16[32,64,128]{2,1,0:T(8,128)(2,1)}, u32[]{:S(2)}, u32[]{:S(2)}) collective-permute-start(bf16[32,64,128]{2,1,0:T(8,128)(2,1)} %get-tuple-element.241), channel_id=1, source_target_pairs={{0,1},{1,2},{2,3},{3,4},{4,5},{5,6},{6,7},{7,8},{8,9},{9,10},{10,1... | collective-permute-start | bytes 1572872 | tf_op jit(solution)/shard_map/while/body/eval_jaxpr/ppermute | solution.py:23
  257.8 8.4 %collective-permute-done = bf16[32,64,128]{2,1,0:T(8,128)(2,1)} collective-permute-done((bf16[32,64,128]{2,1,0:T(8,128)(2,1)}, bf16[32,64,128]{2,1,0:T(8,128)(2,1)}, u32[]{:S(2)}, u32[]{:S(2)}) %collective-permute-start) | collective-permute-done | bytes 524320 | tf_op jit(solution)/shard_map/while/body/eval_jaxpr/ppermute | solution.py:23
  270.9 11.1 %collective-permute-start = (bf16[32,64,128]{2,1,0:T(8,128)(2,1)}, bf16[32,64,128]{2,1,0:T(8,128)(2,1)}, u32[]{:S(2)}, u32[]{:S(2)}) collective-permute-start(bf16[32,64,128]{2,1,0:T(8,128)(2,1)} %get-tuple-element.241), channel_id=1, source_target_pairs={{0,1},{1,2},{2,3},{3,4},{4,5},{5,6},{6,7},{7,8},{8,9},{9,10},{10,1... | collective-permute-start | bytes 1572872 | tf_op jit(solution)/shard_map/while/body/eval_jaxpr/ppermute | solution.py:23
  282.0 6.9 collective-permute-done
  293.5 11.7 %collective-permute-start = (bf16[32,64,128]{2,1,0:T(8,128)(2,1)}, bf16[32,64,128]{2,1,0:T(8,128)(2,1)}, u32[]{:S(2)}, u32[]{:S(2)}) collective-permute-start(bf16[32,64,128]{2,1,0:T(8,128)(2,1)} %get-tuple-element.241), channel_id=1, source_target_pairs={{0,1},{1,2},{2,3},{3,4},{4,5},{5,6},{6,7},{7,8},{8,9},{9,10},{10,1... | collective-permute-start | bytes 1572872 | tf_op jit(solution)/shard_map/while/body/eval_jaxpr/ppermute | solution.py:23
  305.3 7.3 collective-permute-done
  317.3 12.3 %collective-permute-start = (bf16[32,64,128]{2,1,0:T(8,128)(2,1)}, bf16[32,64,128]{2,1,0:T(8,128)(2,1)}, u32[]{:S(2)}, u32[]{:S(2)}) collective-permute-start(bf16[32,64,128]{2,1,0:T(8,128)(2,1)} %get-tuple-element.241), channel_id=1, source_target_pairs={{0,1},{1,2},{2,3},{3,4},{4,5},{5,6},{6,7},{7,8},{8,9},{9,10},{10,1... | collective-permute-start | bytes 1572872 | tf_op jit(solution)/shard_map/while/body/eval_jaxpr/ppermute | solution.py:23
  329.6 8.0 %collective-permute-done = bf16[32,64,128]{2,1,0:T(8,128)(2,1)} collective-permute-done((bf16[32,64,128]{2,1,0:T(8,128)(2,1)}, bf16[32,64,128]{2,1,0:T(8,128)(2,1)}, u32[]{:S(2)}, u32[]{:S(2)}) %collective-permute-start) | collective-permute-done | bytes 524320 | tf_op jit(solution)/shard_map/while/body/eval_jaxpr/ppermute | solution.py:23
  342.3 11.3 %collective-permute-start = (bf16[32,64,128]{2,1,0:T(8,128)(2,1)}, bf16[32,64,128]{2,1,0:T(8,128)(2,1)}, u32[]{:S(2)}, u32[]{:S(2)}) collective-permute-start(bf16[32,64,128]{2,1,0:T(8,128)(2,1)} %get-tuple-element.241), channel_id=1, source_target_pairs={{0,1},{1,2},{2,3},{3,4},{4,5},{5,6},{6,7},{7,8},{8,9},{9,10},{10,1... | collective-permute-start | bytes 1572872 | tf_op jit(solution)/shard_map/while/body/eval_jaxpr/ppermute | solution.py:23
  353.6 9.6 %collective-permute-done = bf16[32,64,128]{2,1,0:T(8,128)(2,1)} collective-permute-done((bf16[32,64,128]{2,1,0:T(8,128)(2,1)}, bf16[32,64,128]{2,1,0:T(8,128)(2,1)}, u32[]{:S(2)}, u32[]{:S(2)}) %collective-permute-start) | collective-permute-done | bytes 524320 | tf_op jit(solution)/shard_map/while/body/eval_jaxpr/ppermute | solution.py:23
  367.9 10.7 %collective-permute-start = (bf16[32,64,128]{2,1,0:T(8,128)(2,1)}, bf16[32,64,128]{2,1,0:T(8,128)(2,1)}, u32[]{:S(2)}, u32[]{:S(2)}) collective-permute-start(bf16[32,64,128]{2,1,0:T(8,128)(2,1)} %get-tuple-element.241), channel_id=1, source_target_pairs={{0,1},{1,2},{2,3},{3,4},{4,5},{5,6},{6,7},{7,8},{8,9},{9,10},{10,1... | collective-permute-start | bytes 1572872 | tf_op jit(solution)/shard_map/while/body/eval_jaxpr/ppermute | solution.py:23
  378.6 9.4 %collective-permute-done = bf16[32,64,128]{2,1,0:T(8,128)(2,1)} collective-permute-done((bf16[32,64,128]{2,1,0:T(8,128)(2,1)}, bf16[32,64,128]{2,1,0:T(8,128)(2,1)}, u32[]{:S(2)}, u32[]{:S(2)}) %collective-permute-start) | collective-permute-done | bytes 524320 | tf_op jit(solution)/shard_map/while/body/eval_jaxpr/ppermute | solution.py:23
  398.4 331.2 %all-reduce.4.cloned.1.call-done = f32[512,96]{0,1:T(8,128)} async-done(((f32[512,96]{0,1:T(8,128)}), f32[512,96]{0,1:T(8,128)}) %all-reduce.4.cloned.1.call-update) | async-done | bytes 196624 | tf_op jit(solution)/shard_map/psum | solution.py:99
  (89 shorter events, 110.3 us)
Async XLA Ops:
  7.2 11.7 %copy-start.7 = (bf16[32,64,128]{2,1,0:T(8,128)(2,1)S(1)}, bf16[32,64,128]{2,1,0:T(8,128)(2,1)}, u32[]{:S(2)}) copy-start(bf16[32,64,128]{2,1,0:T(8,128)(2,1)} %param.10) | copy-start | bytes 1572868
  7.2 722.4 %all-reduce.4.cloned.1.call-start = ((), (), s32[]{:S(2)}) async-start(), calls=%async_computation | async-start | bytes 393216 | tf_op jit(solution)/shard_map/psum | solution.py:99
  8.3 12.2 %copy-start.8 = (bf16[32,64,128]{2,1,0:T(8,128)(2,1)}, bf16[32,64,128]{2,1,0:T(8,128)(2,1)S(1)}, u32[]{:S(2)}) copy-start(bf16[32,64,128]{2,1,0:T(8,128)(2,1)S(1)} %copy.128) | copy-start | bytes 1572868
  12.3 10.8 %collective-permute-start.2 = (bf16[33,64,2]{1,2,0:T(2,128)(2,1)S(1)}, bf16[33,64,2]{1,2,0:T(2,128)(2,1)S(1)}, u32[]{:S(2)}, u32[]{:S(2)}) collective-permute-start(bf16[33,64,2]{1,2,0:T(2,128)(2,1)S(1)} %copy.104), channel_id=1, source_target_pairs={{16,0},{32,16},{48,32},{64,48},{80,64},{96,80},{112,96},{128,112},... | collective-permute-start | bytes 25352 | tf_op jit(solution)/shard_map/ppermute | solution.py:15
  13.9 9.2 %collective-permute-start.1 = (bf16[33,64,2]{1,2,0:T(2,128)(2,1)S(1)}, bf16[33,64,2]{1,2,0:T(2,128)(2,1)S(1)}, u32[]{:S(2)}, u32[]{:S(2)}) collective-permute-start(bf16[33,64,2]{1,2,0:T(2,128)(2,1)S(1)} %copy.103), channel_id=1, source_target_pairs={{0,16},{16,32},{32,48},{48,64},{64,80},{80,96},{96,112},{112,128},... | collective-permute-start | bytes 25352 | tf_op jit(solution)/shard_map/ppermute | solution.py:14
  32.3 2.2 copy-start
  32.3 2.4 copy-start.2
  34.6 1.3 copy-start.4
  46.0 4.3 copy-start.1
  46.0 4.3 copy-start.3
  46.0 4.3 copy-start.5
  55.8 16.7 %collective-permute-start = (bf16[32,64,128]{2,1,0:T(8,128)(2,1)}, bf16[32,64,128]{2,1,0:T(8,128)(2,1)}, u32[]{:S(2)}, u32[]{:S(2)}) collective-permute-start(bf16[32,64,128]{2,1,0:T(8,128)(2,1)} %get-tuple-element.241), channel_id=1, source_target_pairs={{0,1},{1,2},{2,3},{3,4},{4,5},{5,6},{6,7},{7,8},{8,9},{9,10},{10,1... | collective-permute-start | bytes 1572872 | tf_op jit(solution)/shard_map/while/body/eval_jaxpr/ppermute | solution.py:23
  77.2 15.6 %collective-permute-start = (bf16[32,64,128]{2,1,0:T(8,128)(2,1)}, bf16[32,64,128]{2,1,0:T(8,128)(2,1)}, u32[]{:S(2)}, u32[]{:S(2)}) collective-permute-start(bf16[32,64,128]{2,1,0:T(8,128)(2,1)} %get-tuple-element.241), channel_id=1, source_target_pairs={{0,1},{1,2},{2,3},{3,4},{4,5},{5,6},{6,7},{7,8},{8,9},{9,10},{10,1... | collective-permute-start | bytes 1572872 | tf_op jit(solution)/shard_map/while/body/eval_jaxpr/ppermute | solution.py:23
  97.4 15.6 %collective-permute-start = (bf16[32,64,128]{2,1,0:T(8,128)(2,1)}, bf16[32,64,128]{2,1,0:T(8,128)(2,1)}, u32[]{:S(2)}, u32[]{:S(2)}) collective-permute-start(bf16[32,64,128]{2,1,0:T(8,128)(2,1)} %get-tuple-element.241), channel_id=1, source_target_pairs={{0,1},{1,2},{2,3},{3,4},{4,5},{5,6},{6,7},{7,8},{8,9},{9,10},{10,1... | collective-permute-start | bytes 1572872 | tf_op jit(solution)/shard_map/while/body/eval_jaxpr/ppermute | solution.py:23
  117.7 15.6 %collective-permute-start = (bf16[32,64,128]{2,1,0:T(8,128)(2,1)}, bf16[32,64,128]{2,1,0:T(8,128)(2,1)}, u32[]{:S(2)}, u32[]{:S(2)}) collective-permute-start(bf16[32,64,128]{2,1,0:T(8,128)(2,1)} %get-tuple-element.241), channel_id=1, source_target_pairs={{0,1},{1,2},{2,3},{3,4},{4,5},{5,6},{6,7},{7,8},{8,9},{9,10},{10,1... | collective-permute-start | bytes 1572872 | tf_op jit(solution)/shard_map/while/body/eval_jaxpr/ppermute | solution.py:23
  137.9 15.6 %collective-permute-start = (bf16[32,64,128]{2,1,0:T(8,128)(2,1)}, bf16[32,64,128]{2,1,0:T(8,128)(2,1)}, u32[]{:S(2)}, u32[]{:S(2)}) collective-permute-start(bf16[32,64,128]{2,1,0:T(8,128)(2,1)} %get-tuple-element.241), channel_id=1, source_target_pairs={{0,1},{1,2},{2,3},{3,4},{4,5},{5,6},{6,7},{7,8},{8,9},{9,10},{10,1... | collective-permute-start | bytes 1572872 | tf_op jit(solution)/shard_map/while/body/eval_jaxpr/ppermute | solution.py:23
  158.2 15.6 %collective-permute-start = (bf16[32,64,128]{2,1,0:T(8,128)(2,1)}, bf16[32,64,128]{2,1,0:T(8,128)(2,1)}, u32[]{:S(2)}, u32[]{:S(2)}) collective-permute-start(bf16[32,64,128]{2,1,0:T(8,128)(2,1)} %get-tuple-element.241), channel_id=1, source_target_pairs={{0,1},{1,2},{2,3},{3,4},{4,5},{5,6},{6,7},{7,8},{8,9},{9,10},{10,1... | collective-permute-start | bytes 1572872 | tf_op jit(solution)/shard_map/while/body/eval_jaxpr/ppermute | solution.py:23
  178.5 15.6 %collective-permute-start = (bf16[32,64,128]{2,1,0:T(8,128)(2,1)}, bf16[32,64,128]{2,1,0:T(8,128)(2,1)}, u32[]{:S(2)}, u32[]{:S(2)}) collective-permute-start(bf16[32,64,128]{2,1,0:T(8,128)(2,1)} %get-tuple-element.241), channel_id=1, source_target_pairs={{0,1},{1,2},{2,3},{3,4},{4,5},{5,6},{6,7},{7,8},{8,9},{9,10},{10,1... | collective-permute-start | bytes 1572872 | tf_op jit(solution)/shard_map/while/body/eval_jaxpr/ppermute | solution.py:23
  198.7 16.1 %collective-permute-start = (bf16[32,64,128]{2,1,0:T(8,128)(2,1)}, bf16[32,64,128]{2,1,0:T(8,128)(2,1)}, u32[]{:S(2)}, u32[]{:S(2)}) collective-permute-start(bf16[32,64,128]{2,1,0:T(8,128)(2,1)} %get-tuple-element.241), channel_id=1, source_target_pairs={{0,1},{1,2},{2,3},{3,4},{4,5},{5,6},{6,7},{7,8},{8,9},{9,10},{10,1... | collective-permute-start | bytes 1572872 | tf_op jit(solution)/shard_map/while/body/eval_jaxpr/ppermute | solution.py:23
  219.6 20.9 %collective-permute-start = (bf16[32,64,128]{2,1,0:T(8,128)(2,1)}, bf16[32,64,128]{2,1,0:T(8,128)(2,1)}, u32[]{:S(2)}, u32[]{:S(2)}) collective-permute-start(bf16[32,64,128]{2,1,0:T(8,128)(2,1)} %get-tuple-element.241), channel_id=1, source_target_pairs={{0,1},{1,2},{2,3},{3,4},{4,5},{5,6},{6,7},{7,8},{8,9},{9,10},{10,1... | collective-permute-start | bytes 1572872 | tf_op jit(solution)/shard_map/while/body/eval_jaxpr/ppermute | solution.py:23
  245.1 21.1 %collective-permute-start = (bf16[32,64,128]{2,1,0:T(8,128)(2,1)}, bf16[32,64,128]{2,1,0:T(8,128)(2,1)}, u32[]{:S(2)}, u32[]{:S(2)}) collective-permute-start(bf16[32,64,128]{2,1,0:T(8,128)(2,1)} %get-tuple-element.241), channel_id=1, source_target_pairs={{0,1},{1,2},{2,3},{3,4},{4,5},{5,6},{6,7},{7,8},{8,9},{9,10},{10,1... | collective-permute-start | bytes 1572872 | tf_op jit(solution)/shard_map/while/body/eval_jaxpr/ppermute | solution.py:23
  270.9 18.0 %collective-permute-start = (bf16[32,64,128]{2,1,0:T(8,128)(2,1)}, bf16[32,64,128]{2,1,0:T(8,128)(2,1)}, u32[]{:S(2)}, u32[]{:S(2)}) collective-permute-start(bf16[32,64,128]{2,1,0:T(8,128)(2,1)} %get-tuple-element.241), channel_id=1, source_target_pairs={{0,1},{1,2},{2,3},{3,4},{4,5},{5,6},{6,7},{7,8},{8,9},{9,10},{10,1... | collective-permute-start | bytes 1572872 | tf_op jit(solution)/shard_map/while/body/eval_jaxpr/ppermute | solution.py:23
  293.5 19.1 %collective-permute-start = (bf16[32,64,128]{2,1,0:T(8,128)(2,1)}, bf16[32,64,128]{2,1,0:T(8,128)(2,1)}, u32[]{:S(2)}, u32[]{:S(2)}) collective-permute-start(bf16[32,64,128]{2,1,0:T(8,128)(2,1)} %get-tuple-element.241), channel_id=1, source_target_pairs={{0,1},{1,2},{2,3},{3,4},{4,5},{5,6},{6,7},{7,8},{8,9},{9,10},{10,1... | collective-permute-start | bytes 1572872 | tf_op jit(solution)/shard_map/while/body/eval_jaxpr/ppermute | solution.py:23
  317.3 20.4 %collective-permute-start = (bf16[32,64,128]{2,1,0:T(8,128)(2,1)}, bf16[32,64,128]{2,1,0:T(8,128)(2,1)}, u32[]{:S(2)}, u32[]{:S(2)}) collective-permute-start(bf16[32,64,128]{2,1,0:T(8,128)(2,1)} %get-tuple-element.241), channel_id=1, source_target_pairs={{0,1},{1,2},{2,3},{3,4},{4,5},{5,6},{6,7},{7,8},{8,9},{9,10},{10,1... | collective-permute-start | bytes 1572872 | tf_op jit(solution)/shard_map/while/body/eval_jaxpr/ppermute | solution.py:23
  342.3 20.9 %collective-permute-start = (bf16[32,64,128]{2,1,0:T(8,128)(2,1)}, bf16[32,64,128]{2,1,0:T(8,128)(2,1)}, u32[]{:S(2)}, u32[]{:S(2)}) collective-permute-start(bf16[32,64,128]{2,1,0:T(8,128)(2,1)} %get-tuple-element.241), channel_id=1, source_target_pairs={{0,1},{1,2},{2,3},{3,4},{4,5},{5,6},{6,7},{7,8},{8,9},{9,10},{10,1... | collective-permute-start | bytes 1572872 | tf_op jit(solution)/shard_map/while/body/eval_jaxpr/ppermute | solution.py:23
  367.9 20.1 %collective-permute-start = (bf16[32,64,128]{2,1,0:T(8,128)(2,1)}, bf16[32,64,128]{2,1,0:T(8,128)(2,1)}, u32[]{:S(2)}, u32[]{:S(2)}) collective-permute-start(bf16[32,64,128]{2,1,0:T(8,128)(2,1)} %get-tuple-element.241), channel_id=1, source_target_pairs={{0,1},{1,2},{2,3},{3,4},{4,5},{5,6},{6,7},{7,8},{8,9},{9,10},{10,1... | collective-permute-start | bytes 1572872 | tf_op jit(solution)/shard_map/while/body/eval_jaxpr/ppermute | solution.py:23
  392.7 3.8 copy-start.6
Sparse Core Ops, SparseCore 0:
  393.6 335.9 all-reduce.3
where the time goes:
time: 740 us; the launch traced here: 738 us
  waiting for transfers between devices  430 us (58%)
  starting transfers between devices  174 us (24%)
  local copies, waits for them, and re-layouts  52.2 us (7%)
  matrix products  47.1 us (6%)
  other arithmetic  19.8 us (3%)
  between operations  14.3 us (2%)
    psum x1, waiting for transfers between devices, local(): total = lax.psum(grams, 'space')  331 us
    ppermute x15, starting transfers between devices, passed_along(): return lax.ppermute(value, axis, pairs)  168 us
    ppermute x15, waiting for transfers between devices, passed_along(): return lax.ppermute(value, axis, pairs)  98.3 us
    dot_general x16, matrix products, place(): lax.dot_general(panel.reshape(panel_size, rows * cols).astype(jnp.float32...  47.1 us
    while x15, local copies, waits for them, and re-layouts  28 us
  transfers between devices with their start and end apart: 18, of which 16 were waited for; matrix products, arithmetic and copies ran while one was open for 1% of the time, Pallas kernels for 0%

commit v1 on v0

--- a/solution.py
+++ b/solution.py
@@ -96,7 +96,7 @@
         return (panel, place(totals, panel, index - step))
 
     last, grams = lax.fori_loop(1, loop_size, turn, (old_modes, grams))
-    total = lax.psum(grams, "space")
+    total = jnp.sum(lax.all_gather(grams, "space"), axis=0)
     cross_mass = total[:, :panel_size] * area
     cross_membrane = total[:, panel_size : 2 * panel_size] * area
     cross_bending = total[:, 2 * panel_size :] * area

time: 740 us -> 642 us (0.87)
  the two profiles are of different devices: /device:TPU:2 before, /device:TPU:4 now
where the time goes in v1:
time: 642 us; the launch traced here: 640 us
  waiting for transfers between devices  348 us (54%)
  starting transfers between devices  153 us (24%)
  local copies, waits for them, and re-layouts  54.4 us (8%)
  matrix products  47.1 us (7%)
  other arithmetic  22.4 us (3%)
  between operations  14.3 us (2%)
    all_gather x1, waiting for transfers between devices, local(): total = jnp.sum(lax.all_gather(grams, 'space'), axis=0)  229 us
    ppermute x15, starting transfers between devices, passed_along(): return lax.ppermute(value, axis, pairs)  147 us
    ppermute x15, waiting for transfers between devices, passed_along(): return lax.ppermute(value, axis, pairs)  118 us
    dot_general x16, matrix products, place(): lax.dot_general(panel.reshape(panel_size, rows * cols).astype(jnp.float32...  47.1 us
    while x15, local copies, waits for them, and re-layouts  28 us
    unnamed x30, local copies, waits for them, and re-layouts  17.6 us
  transfers between devices with their start and end apart: 18, of which 16 were waited for; matrix products, arithmetic and copies ran while one was open for 1% of the time, Pallas kernels for 0%

profile of v1, /device:TPU:4, one launch (start us, length us, event | category | flops | bytes accessed | tf_op | source)
XLA Modules:
  0.0 639.5 jit_solution(9209838769536693478)
XLA Ops:
  13.9 4.9 collective-permute-start.1
  24.7 7.6 %add_convert_fusion = (bf16[32,64,128]{1,0,2:T(8,128)(2,1)}, f32[32,64,128]{1,0,2:T(8,128)S(1)}, f32[32,64,128]{1,0,2:T(8,128)S(1)}, f32[32,64,128]{1,0,2:T(8,128)S(1)}) fusion(f32[32,68,132]{1,0,2:T(8,128)S(1)} %slice_convert_fusion, f32[64,128]{0,1:T(8,128)S(1)} %copy.97, f32[64,128]{0,1:T(8,128)S(1)} %copy.95, f32[64,128]{0,1:T(8,128)S(1)} %copy.92, ...), kind=kLoop, calls=%fused_computation.18 | loop fusion | flops 7602176 | bytes 17465344 | tf_op jit(solution)/shard_map/convert_element_type | solution.py:73
  39.2 6.8 %copy.101 = f32[96,64,128]{2,1,0:T(8,128)} copy(f32[96,64,128]{1,0,2:T(8,128)} %pad_maximum_fusion) | data formatting | bytes 6291456 | tf_op jit(solution)/shard_map/concatenate | solution.py:74
  46.0 4.3 copy.118
  50.3 5.5 fusion.12
  55.8 335.4 %while.17 = (s32[]{:T(128)}, bf16[32,64,128]{2,1,0:T(8,128)(2,1)}, f32[512,96]{1,0:T(8,128)S(1)}, f32[96,8192]{1,0:T(8,128)S(1)}, s32[]{:T(128)}, /*index=5*/s32...) while((s32[]{:T(128)}, bf16[32,64,128]{2,1,0:T(8,128)(2,1)}, ...), condition=%wide.region_5.6_spmd, body=%wide.region_4.5_spmd.sunk | while | flops 301989920 | bytes 6832448 | solution.py:98
  57.8 14.7 %collective-permute-done = bf16[32,64,128]{2,1,0:T(8,128)(2,1)} collective-permute-done((bf16[32,64,128]{2,1,0:T(8,128)(2,1)}, bf16[32,64,128]{2,1,0:T(8,128)(2,1)}, u32[]{:S(2)}, u32[]{:S(2)}) %collective-permute-start) | collective-permute-done | bytes 524320 | tf_op jit(solution)/shard_map/while/body/eval_jaxpr/ppermute | solution.py:23
  77.1 7.9 %collective-permute-start = (bf16[32,64,128]{2,1,0:T(8,128)(2,1)}, bf16[32,64,128]{2,1,0:T(8,128)(2,1)}, u32[]{:S(2)}, u32[]{:S(2)}) collective-permute-start(bf16[32,64,128]{2,1,0:T(8,128)(2,1)} %get-tuple-element.241), channel_id=1, source_target_pairs={{0,1},{1,2},{2,3},{3,4},{4,5},{5,6},{6,7},{7,8},{8,9},{9,10},{10,1... | collective-permute-start | bytes 1572872 | tf_op jit(solution)/shard_map/while/body/eval_jaxpr/ppermute | solution.py:23
  85.0 7.7 %collective-permute-done = bf16[32,64,128]{2,1,0:T(8,128)(2,1)} collective-permute-done((bf16[32,64,128]{2,1,0:T(8,128)(2,1)}, bf16[32,64,128]{2,1,0:T(8,128)(2,1)}, u32[]{:S(2)}, u32[]{:S(2)}) %collective-permute-start) | collective-permute-done | bytes 524320 | tf_op jit(solution)/shard_map/while/body/eval_jaxpr/ppermute | solution.py:23
  97.4 12.3 %collective-permute-start = (bf16[32,64,128]{2,1,0:T(8,128)(2,1)}, bf16[32,64,128]{2,1,0:T(8,128)(2,1)}, u32[]{:S(2)}, u32[]{:S(2)}) collective-permute-start(bf16[32,64,128]{2,1,0:T(8,128)(2,1)} %get-tuple-element.241), channel_id=1, source_target_pairs={{0,1},{1,2},{2,3},{3,4},{4,5},{5,6},{6,7},{7,8},{8,9},{9,10},{10,1... | collective-permute-start | bytes 1572872 | tf_op jit(solution)/shard_map/while/body/eval_jaxpr/ppermute | solution.py:23
  117.7 12.4 %collective-permute-start = (bf16[32,64,128]{2,1,0:T(8,128)(2,1)}, bf16[32,64,128]{2,1,0:T(8,128)(2,1)}, u32[]{:S(2)}, u32[]{:S(2)}) collective-permute-start(bf16[32,64,128]{2,1,0:T(8,128)(2,1)} %get-tuple-element.241), channel_id=1, source_target_pairs={{0,1},{1,2},{2,3},{3,4},{4,5},{5,6},{6,7},{7,8},{8,9},{9,10},{10,1... | collective-permute-start | bytes 1572872 | tf_op jit(solution)/shard_map/while/body/eval_jaxpr/ppermute | solution.py:23
  137.9 12.5 %collective-permute-start = (bf16[32,64,128]{2,1,0:T(8,128)(2,1)}, bf16[32,64,128]{2,1,0:T(8,128)(2,1)}, u32[]{:S(2)}, u32[]{:S(2)}) collective-permute-start(bf16[32,64,128]{2,1,0:T(8,128)(2,1)} %get-tuple-element.241), channel_id=1, source_target_pairs={{0,1},{1,2},{2,3},{3,4},{4,5},{5,6},{6,7},{7,8},{8,9},{9,10},{10,1... | collective-permute-start | bytes 1572872 | tf_op jit(solution)/shard_map/while/body/eval_jaxpr/ppermute | solution.py:23
  158.2 12.6 %collective-permute-start = (bf16[32,64,128]{2,1,0:T(8,128)(2,1)}, bf16[32,64,128]{2,1,0:T(8,128)(2,1)}, u32[]{:S(2)}, u32[]{:S(2)}) collective-permute-start(bf16[32,64,128]{2,1,0:T(8,128)(2,1)} %get-tuple-element.241), channel_id=1, source_target_pairs={{0,1},{1,2},{2,3},{3,4},{4,5},{5,6},{6,7},{7,8},{8,9},{9,10},{10,1... | collective-permute-start | bytes 1572872 | tf_op jit(solution)/shard_map/while/body/eval_jaxpr/ppermute | solution.py:23
  178.5 12.6 %collective-permute-start = (bf16[32,64,128]{2,1,0:T(8,128)(2,1)}, bf16[32,64,128]{2,1,0:T(8,128)(2,1)}, u32[]{:S(2)}, u32[]{:S(2)}) collective-permute-start(bf16[32,64,128]{2,1,0:T(8,128)(2,1)} %get-tuple-element.241), channel_id=1, source_target_pairs={{0,1},{1,2},{2,3},{3,4},{4,5},{5,6},{6,7},{7,8},{8,9},{9,10},{10,1... | collective-permute-start | bytes 1572872 | tf_op jit(solution)/shard_map/while/body/eval_jaxpr/ppermute | solution.py:23
  191.1 8.7 %collective-permute-done = bf16[32,64,128]{2,1,0:T(8,128)(2,1)} collective-permute-done((bf16[32,64,128]{2,1,0:T(8,128)(2,1)}, bf16[32,64,128]{2,1,0:T(8,128)(2,1)}, u32[]{:S(2)}, u32[]{:S(2)}) %collective-permute-start) | collective-permute-done | bytes 524320 | tf_op jit(solution)/shard_map/while/body/eval_jaxpr/ppermute | solution.py:23
  204.4 7.0 %collective-permute-start = (bf16[32,64,128]{2,1,0:T(8,128)(2,1)}, bf16[32,64,128]{2,1,0:T(8,128)(2,1)}, u32[]{:S(2)}, u32[]{:S(2)}) collective-permute-start(bf16[32,64,128]{2,1,0:T(8,128)(2,1)} %get-tuple-element.241), channel_id=1, source_target_pairs={{0,1},{1,2},{2,3},{3,4},{4,5},{5,6},{6,7},{7,8},{8,9},{9,10},{10,1... | collective-permute-start | bytes 1572872 | tf_op jit(solution)/shard_map/while/body/eval_jaxpr/ppermute | solution.py:23
  211.5 12.9 %collective-permute-done = bf16[32,64,128]{2,1,0:T(8,128)(2,1)} collective-permute-done((bf16[32,64,128]{2,1,0:T(8,128)(2,1)}, bf16[32,64,128]{2,1,0:T(8,128)(2,1)}, u32[]{:S(2)}, u32[]{:S(2)}) %collective-permute-start) | collective-permute-done | bytes 524320 | tf_op jit(solution)/shard_map/while/body/eval_jaxpr/ppermute | solution.py:23
  232.7 12.1 %collective-permute-done = bf16[32,64,128]{2,1,0:T(8,128)(2,1)} collective-permute-done((bf16[32,64,128]{2,1,0:T(8,128)(2,1)}, bf16[32,64,128]{2,1,0:T(8,128)(2,1)}, u32[]{:S(2)}, u32[]{:S(2)}) %collective-permute-start) | collective-permute-done | bytes 524320 | tf_op jit(solution)/shard_map/while/body/eval_jaxpr/ppermute | solution.py:23
  249.5 8.2 %collective-permute-start = (bf16[32,64,128]{2,1,0:T(8,128)(2,1)}, bf16[32,64,128]{2,1,0:T(8,128)(2,1)}, u32[]{:S(2)}, u32[]{:S(2)}) collective-permute-start(bf16[32,64,128]{2,1,0:T(8,128)(2,1)} %get-tuple-element.241), channel_id=1, source_target_pairs={{0,1},{1,2},{2,3},{3,4},{4,5},{5,6},{6,7},{7,8},{8,9},{9,10},{10,1... | collective-permute-start | bytes 1572872 | tf_op jit(solution)/shard_map/while/body/eval_jaxpr/ppermute | solution.py:23
  257.7 7.4 %collective-permute-done = bf16[32,64,128]{2,1,0:T(8,128)(2,1)} collective-permute-done((bf16[32,64,128]{2,1,0:T(8,128)(2,1)}, bf16[32,64,128]{2,1,0:T(8,128)(2,1)}, u32[]{:S(2)}, u32[]{:S(2)}) %collective-permute-start) | collective-permute-done | bytes 524320 | tf_op jit(solution)/shard_map/while/body/eval_jaxpr/ppermute | solution.py:23
  269.7 12.3 %collective-permute-start = (bf16[32,64,128]{2,1,0:T(8,128)(2,1)}, bf16[32,64,128]{2,1,0:T(8,128)(2,1)}, u32[]{:S(2)}, u32[]{:S(2)}) collective-permute-start(bf16[32,64,128]{2,1,0:T(8,128)(2,1)} %get-tuple-element.241), channel_id=1, source_target_pairs={{0,1},{1,2},{2,3},{3,4},{4,5},{5,6},{6,7},{7,8},{8,9},{9,10},{10,1... | collective-permute-start | bytes 1572872 | tf_op jit(solution)/shard_map/while/body/eval_jaxpr/ppermute | solution.py:23
  282.1 6.3 collective-permute-done
  293.0 12.0 %collective-permute-start = (bf16[32,64,128]{2,1,0:T(8,128)(2,1)}, bf16[32,64,128]{2,1,0:T(8,128)(2,1)}, u32[]{:S(2)}, u32[]{:S(2)}) collective-permute-start(bf16[32,64,128]{2,1,0:T(8,128)(2,1)} %get-tuple-element.241), channel_id=1, source_target_pairs={{0,1},{1,2},{2,3},{3,4},{4,5},{5,6},{6,7},{7,8},{8,9},{9,10},{10,1... | collective-permute-start | bytes 1572872 | tf_op jit(solution)/shard_map/while/body/eval_jaxpr/ppermute | solution.py:23
  305.1 8.4 %collective-permute-done = bf16[32,64,128]{2,1,0:T(8,128)(2,1)} collective-permute-done((bf16[32,64,128]{2,1,0:T(8,128)(2,1)}, bf16[32,64,128]{2,1,0:T(8,128)(2,1)}, u32[]{:S(2)}, u32[]{:S(2)}) %collective-permute-start) | collective-permute-done | bytes 524320 | tf_op jit(solution)/shard_map/while/body/eval_jaxpr/ppermute | solution.py:23
  318.1 11.2 %collective-permute-start = (bf16[32,64,128]{2,1,0:T(8,128)(2,1)}, bf16[32,64,128]{2,1,0:T(8,128)(2,1)}, u32[]{:S(2)}, u32[]{:S(2)}) collective-permute-start(bf16[32,64,128]{2,1,0:T(8,128)(2,1)} %get-tuple-element.241), channel_id=1, source_target_pairs={{0,1},{1,2},{2,3},{3,4},{4,5},{5,6},{6,7},{7,8},{8,9},{9,10},{10,1... | collective-permute-start | bytes 1572872 | tf_op jit(solution)/shard_map/while/body/eval_jaxpr/ppermute | solution.py:23
  329.4 9.7 %collective-permute-done = bf16[32,64,128]{2,1,0:T(8,128)(2,1)} collective-permute-done((bf16[32,64,128]{2,1,0:T(8,128)(2,1)}, bf16[32,64,128]{2,1,0:T(8,128)(2,1)}, u32[]{:S(2)}, u32[]{:S(2)}) %collective-permute-start) | collective-permute-done | bytes 524320 | tf_op jit(solution)/shard_map/while/body/eval_jaxpr/ppermute | solution.py:23
  343.7 9.7 %collective-permute-start = (bf16[32,64,128]{2,1,0:T(8,128)(2,1)}, bf16[32,64,128]{2,1,0:T(8,128)(2,1)}, u32[]{:S(2)}, u32[]{:S(2)}) collective-permute-start(bf16[32,64,128]{2,1,0:T(8,128)(2,1)} %get-tuple-element.241), channel_id=1, source_target_pairs={{0,1},{1,2},{2,3},{3,4},{4,5},{5,6},{6,7},{7,8},{8,9},{9,10},{10,1... | collective-permute-start | bytes 1572872 | tf_op jit(solution)/shard_map/while/body/eval_jaxpr/ppermute | solution.py:23
  353.4 9.8 %collective-permute-done = bf16[32,64,128]{2,1,0:T(8,128)(2,1)} collective-permute-done((bf16[32,64,128]{2,1,0:T(8,128)(2,1)}, bf16[32,64,128]{2,1,0:T(8,128)(2,1)}, u32[]{:S(2)}, u32[]{:S(2)}) %collective-permute-start) | collective-permute-done | bytes 524320 | tf_op jit(solution)/shard_map/while/body/eval_jaxpr/ppermute | solution.py:23
  367.9 10.5 %collective-permute-start = (bf16[32,64,128]{2,1,0:T(8,128)(2,1)}, bf16[32,64,128]{2,1,0:T(8,128)(2,1)}, u32[]{:S(2)}, u32[]{:S(2)}) collective-permute-start(bf16[32,64,128]{2,1,0:T(8,128)(2,1)} %get-tuple-element.241), channel_id=1, source_target_pairs={{0,1},{1,2},{2,3},{3,4},{4,5},{5,6},{6,7},{7,8},{8,9},{9,10},{10,1... | collective-permute-start | bytes 1572872 | tf_op jit(solution)/shard_map/while/body/eval_jaxpr/ppermute | solution.py:23
  378.5 8.1 %collective-permute-done = bf16[32,64,128]{2,1,0:T(8,128)(2,1)} collective-permute-done((bf16[32,64,128]{2,1,0:T(8,128)(2,1)}, bf16[32,64,128]{2,1,0:T(8,128)(2,1)}, u32[]{:S(2)}, u32[]{:S(2)}) %collective-permute-start) | collective-permute-done | bytes 524320 | tf_op jit(solution)/shard_map/while/body/eval_jaxpr/ppermute | solution.py:23
  396.9 229.4 %all-gather.3.cloned.1.call-done = f32[16384,96]{1,0:T(8,128)} async-done(((f32[512,96]{1,0:T(8,128)}), f32[16384,96]{1,0:T(8,128)}) %all-gather.3.cloned.1.call-update) | async-done | bytes 6291472 | tf_op jit(solution)/shard_map/all_gather | solution.py:99
  626.2 4.0 reduce_sum.49
  (94 shorter events, 115.2 us)
Async XLA Ops:
  7.2 11.7 %copy-start.7 = (bf16[32,64,128]{2,1,0:T(8,128)(2,1)S(1)}, bf16[32,64,128]{2,1,0:T(8,128)(2,1)}, u32[]{:S(2)}) copy-start(bf16[32,64,128]{2,1,0:T(8,128)(2,1)} %param.10) | copy-start | bytes 1572868
  7.2 619.0 %all-gather.3.cloned.1.call-start = ((), (), s32[]{:S(2)}) async-start(), calls=%async_computation | async-start | bytes 8650752 | tf_op jit(solution)/shard_map/all_gather | solution.py:99
  8.3 12.2 %copy-start.8 = (bf16[32,64,128]{2,1,0:T(8,128)(2,1)}, bf16[32,64,128]{2,1,0:T(8,128)(2,1)S(1)}, u32[]{:S(2)}) copy-start(bf16[32,64,128]{2,1,0:T(8,128)(2,1)S(1)} %copy.133) | copy-start | bytes 1572868
  12.3 10.8 %collective-permute-start.2 = (bf16[33,64,2]{1,2,0:T(2,128)(2,1)S(1)}, bf16[33,64,2]{1,2,0:T(2,128)(2,1)S(1)}, u32[]{:S(2)}, u32[]{:S(2)}) collective-permute-start(bf16[33,64,2]{1,2,0:T(2,128)(2,1)S(1)} %copy.110), channel_id=1, source_target_pairs={{16,0},{32,16},{48,32},{64,48},{80,64},{96,80},{112,96},{128,112},... | collective-permute-start | bytes 25352 | tf_op jit(solution)/shard_map/ppermute | solution.py:15
  13.9 9.2 %collective-permute-start.1 = (bf16[33,64,2]{1,2,0:T(2,128)(2,1)S(1)}, bf16[33,64,2]{1,2,0:T(2,128)(2,1)S(1)}, u32[]{:S(2)}, u32[]{:S(2)}) collective-permute-start(bf16[33,64,2]{1,2,0:T(2,128)(2,1)S(1)} %copy.109), channel_id=1, source_target_pairs={{0,16},{16,32},{32,48},{48,64},{64,80},{80,96},{96,112},{112,128},... | collective-permute-start | bytes 25352 | tf_op jit(solution)/shard_map/ppermute | solution.py:14
  32.3 2.2 copy-start
  32.3 2.4 copy-start.2
  34.6 1.3 copy-start.4
  46.0 4.3 copy-start.1
  46.0 4.3 copy-start.3
  46.0 4.3 copy-start.5
  55.8 16.7 %collective-permute-start = (bf16[32,64,128]{2,1,0:T(8,128)(2,1)}, bf16[32,64,128]{2,1,0:T(8,128)(2,1)}, u32[]{:S(2)}, u32[]{:S(2)}) collective-permute-start(bf16[32,64,128]{2,1,0:T(8,128)(2,1)} %get-tuple-element.241), channel_id=1, source_target_pairs={{0,1},{1,2},{2,3},{3,4},{4,5},{5,6},{6,7},{7,8},{8,9},{9,10},{10,1... | collective-permute-start | bytes 1572872 | tf_op jit(solution)/shard_map/while/body/eval_jaxpr/ppermute | solution.py:23
  77.1 15.6 %collective-permute-start = (bf16[32,64,128]{2,1,0:T(8,128)(2,1)}, bf16[32,64,128]{2,1,0:T(8,128)(2,1)}, u32[]{:S(2)}, u32[]{:S(2)}) collective-permute-start(bf16[32,64,128]{2,1,0:T(8,128)(2,1)} %get-tuple-element.241), channel_id=1, source_target_pairs={{0,1},{1,2},{2,3},{3,4},{4,5},{5,6},{6,7},{7,8},{8,9},{9,10},{10,1... | collective-permute-start | bytes 1572872 | tf_op jit(solution)/shard_map/while/body/eval_jaxpr/ppermute | solution.py:23
  97.4 15.6 %collective-permute-start = (bf16[32,64,128]{2,1,0:T(8,128)(2,1)}, bf16[32,64,128]{2,1,0:T(8,128)(2,1)}, u32[]{:S(2)}, u32[]{:S(2)}) collective-permute-start(bf16[32,64,128]{2,1,0:T(8,128)(2,1)} %get-tuple-element.241), channel_id=1, source_target_pairs={{0,1},{1,2},{2,3},{3,4},{4,5},{5,6},{6,7},{7,8},{8,9},{9,10},{10,1... | collective-permute-start | bytes 1572872 | tf_op jit(solution)/shard_map/while/body/eval_jaxpr/ppermute | solution.py:23
  117.7 15.6 %collective-permute-start = (bf16[32,64,128]{2,1,0:T(8,128)(2,1)}, bf16[32,64,128]{2,1,0:T(8,128)(2,1)}, u32[]{:S(2)}, u32[]{:S(2)}) collective-permute-start(bf16[32,64,128]{2,1,0:T(8,128)(2,1)} %get-tuple-element.241), channel_id=1, source_target_pairs={{0,1},{1,2},{2,3},{3,4},{4,5},{5,6},{6,7},{7,8},{8,9},{9,10},{10,1... | collective-permute-start | bytes 1572872 | tf_op jit(solution)/shard_map/while/body/eval_jaxpr/ppermute | solution.py:23
  137.9 15.6 %collective-permute-start = (bf16[32,64,128]{2,1,0:T(8,128)(2,1)}, bf16[32,64,128]{2,1,0:T(8,128)(2,1)}, u32[]{:S(2)}, u32[]{:S(2)}) collective-permute-start(bf16[32,64,128]{2,1,0:T(8,128)(2,1)} %get-tuple-element.241), channel_id=1, source_target_pairs={{0,1},{1,2},{2,3},{3,4},{4,5},{5,6},{6,7},{7,8},{8,9},{9,10},{10,1... | collective-permute-start | bytes 1572872 | tf_op jit(solution)/shard_map/while/body/eval_jaxpr/ppermute | solution.py:23
  158.2 15.6 %collective-permute-start = (bf16[32,64,128]{2,1,0:T(8,128)(2,1)}, bf16[32,64,128]{2,1,0:T(8,128)(2,1)}, u32[]{:S(2)}, u32[]{:S(2)}) collective-permute-start(bf16[32,64,128]{2,1,0:T(8,128)(2,1)} %get-tuple-element.241), channel_id=1, source_target_pairs={{0,1},{1,2},{2,3},{3,4},{4,5},{5,6},{6,7},{7,8},{8,9},{9,10},{10,1... | collective-permute-start | bytes 1572872 | tf_op jit(solution)/shard_map/while/body/eval_jaxpr/ppermute | solution.py:23
  178.5 21.3 %collective-permute-start = (bf16[32,64,128]{2,1,0:T(8,128)(2,1)}, bf16[32,64,128]{2,1,0:T(8,128)(2,1)}, u32[]{:S(2)}, u32[]{:S(2)}) collective-permute-start(bf16[32,64,128]{2,1,0:T(8,128)(2,1)} %get-tuple-element.241), channel_id=1, source_target_pairs={{0,1},{1,2},{2,3},{3,4},{4,5},{5,6},{6,7},{7,8},{8,9},{9,10},{10,1... | collective-permute-start | bytes 1572872 | tf_op jit(solution)/shard_map/while/body/eval_jaxpr/ppermute | solution.py:23
  204.4 20.0 %collective-permute-start = (bf16[32,64,128]{2,1,0:T(8,128)(2,1)}, bf16[32,64,128]{2,1,0:T(8,128)(2,1)}, u32[]{:S(2)}, u32[]{:S(2)}) collective-permute-start(bf16[32,64,128]{2,1,0:T(8,128)(2,1)} %get-tuple-element.241), channel_id=1, source_target_pairs={{0,1},{1,2},{2,3},{3,4},{4,5},{5,6},{6,7},{7,8},{8,9},{9,10},{10,1... | collective-permute-start | bytes 1572872 | tf_op jit(solution)/shard_map/while/body/eval_jaxpr/ppermute | solution.py:23
  229.1 15.7 %collective-permute-start = (bf16[32,64,128]{2,1,0:T(8,128)(2,1)}, bf16[32,64,128]{2,1,0:T(8,128)(2,1)}, u32[]{:S(2)}, u32[]{:S(2)}) collective-permute-start(bf16[32,64,128]{2,1,0:T(8,128)(2,1)} %get-tuple-element.241), channel_id=1, source_target_pairs={{0,1},{1,2},{2,3},{3,4},{4,5},{5,6},{6,7},{7,8},{8,9},{9,10},{10,1... | collective-permute-start | bytes 1572872 | tf_op jit(solution)/shard_map/while/body/eval_jaxpr/ppermute | solution.py:23
  249.5 15.6 %collective-permute-start = (bf16[32,64,128]{2,1,0:T(8,128)(2,1)}, bf16[32,64,128]{2,1,0:T(8,128)(2,1)}, u32[]{:S(2)}, u32[]{:S(2)}) collective-permute-start(bf16[32,64,128]{2,1,0:T(8,128)(2,1)} %get-tuple-element.241), channel_id=1, source_target_pairs={{0,1},{1,2},{2,3},{3,4},{4,5},{5,6},{6,7},{7,8},{8,9},{9,10},{10,1... | collective-permute-start | bytes 1572872 | tf_op jit(solution)/shard_map/while/body/eval_jaxpr/ppermute | solution.py:23
  269.7 18.6 %collective-permute-start = (bf16[32,64,128]{2,1,0:T(8,128)(2,1)}, bf16[32,64,128]{2,1,0:T(8,128)(2,1)}, u32[]{:S(2)}, u32[]{:S(2)}) collective-permute-start(bf16[32,64,128]{2,1,0:T(8,128)(2,1)} %get-tuple-element.241), channel_id=1, source_target_pairs={{0,1},{1,2},{2,3},{3,4},{4,5},{5,6},{6,7},{7,8},{8,9},{9,10},{10,1... | collective-permute-start | bytes 1572872 | tf_op jit(solution)/shard_map/while/body/eval_jaxpr/ppermute | solution.py:23
  293.0 20.5 %collective-permute-start = (bf16[32,64,128]{2,1,0:T(8,128)(2,1)}, bf16[32,64,128]{2,1,0:T(8,128)(2,1)}, u32[]{:S(2)}, u32[]{:S(2)}) collective-permute-start(bf16[32,64,128]{2,1,0:T(8,128)(2,1)} %get-tuple-element.241), channel_id=1, source_target_pairs={{0,1},{1,2},{2,3},{3,4},{4,5},{5,6},{6,7},{7,8},{8,9},{9,10},{10,1... | collective-permute-start | bytes 1572872 | tf_op jit(solution)/shard_map/while/body/eval_jaxpr/ppermute | solution.py:23
  318.1 21.0 %collective-permute-start = (bf16[32,64,128]{2,1,0:T(8,128)(2,1)}, bf16[32,64,128]{2,1,0:T(8,128)(2,1)}, u32[]{:S(2)}, u32[]{:S(2)}) collective-permute-start(bf16[32,64,128]{2,1,0:T(8,128)(2,1)} %get-tuple-element.241), channel_id=1, source_target_pairs={{0,1},{1,2},{2,3},{3,4},{4,5},{5,6},{6,7},{7,8},{8,9},{9,10},{10,1... | collective-permute-start | bytes 1572872 | tf_op jit(solution)/shard_map/while/body/eval_jaxpr/ppermute | solution.py:23
  343.7 19.5 %collective-permute-start = (bf16[32,64,128]{2,1,0:T(8,128)(2,1)}, bf16[32,64,128]{2,1,0:T(8,128)(2,1)}, u32[]{:S(2)}, u32[]{:S(2)}) collective-permute-start(bf16[32,64,128]{2,1,0:T(8,128)(2,1)} %get-tuple-element.241), channel_id=1, source_target_pairs={{0,1},{1,2},{2,3},{3,4},{4,5},{5,6},{6,7},{7,8},{8,9},{9,10},{10,1... | collective-permute-start | bytes 1572872 | tf_op jit(solution)/shard_map/while/body/eval_jaxpr/ppermute | solution.py:23
  367.9 18.6 %collective-permute-start = (bf16[32,64,128]{2,1,0:T(8,128)(2,1)}, bf16[32,64,128]{2,1,0:T(8,128)(2,1)}, u32[]{:S(2)}, u32[]{:S(2)}) collective-permute-start(bf16[32,64,128]{2,1,0:T(8,128)(2,1)} %get-tuple-element.241), channel_id=1, source_target_pairs={{0,1},{1,2},{2,3},{3,4},{4,5},{5,6},{6,7},{7,8},{8,9},{9,10},{10,1... | collective-permute-start | bytes 1572872 | tf_op jit(solution)/shard_map/while/body/eval_jaxpr/ppermute | solution.py:23
  391.2 0.7 copy-start.9
  391.2 3.8 copy-start.6
Sparse Core Ops, SparseCore 0:
  392.1 234.0 all-gather.2
